TPU v7x, 32 devices: a whole 2x2x4 slice. The times are simulated.
32 devices in a mesh: grp: 2 (over y), fit: 8 (over z, core), occ: 2 (over x), sub: 1.
Axes of the slice: x: 2, y: 2, z: 4, core: 2. Of those that a mesh axis runs over, the one named last changes fastest.
Arguments:
- tiles: bfloat16 [192, 3, 64, 8192], P(('grp', 'fit'), None, None, ('occ', 'sub')), parts along dimension 0, may hold values from -0.015625 to 0.015625
- metric: bfloat16 [192, 64, 64], P(('grp', 'fit')), parts along dimension 0, may hold values from -1 to 2, as said below
- owners: int32 [192, 3], P(('grp', 'fit')), parts along dimension 0, may hold values from 0 to 7, all different within a row; in each aligned block of 12 rows (0 to 11, 12 to 23, ...) at most 9 rows name the same one
Outputs:
- exchange_blocks: bfloat16 [16, 128, 128], P(('grp', 'fit'), ('occ', 'sub')), parts along dimension 0
There are 2 independent parts, one for each index of `grp`. A program takes and returns all parts, laid end to end along the dimension named above; each array names one. Nothing has to cross between parts.
Inputs may be any that keep to these rules, and one draw needn't show every extreme that they name: Each row names 3 different owners. Among the 12 rows of one index of fit no owner is named more than 9 times, and in some such block one owner is named exactly 9 times. `metric`: each tile is lower triangular with a positive diagonal of at most 2.
All inputs are finite; a program needn't handle non-finite values.
Results may differ from a plain program's by a relative error of at most 0.0065.
Values may be sent and summed in bfloat16 or wider, within the bound.
A program may use at most 128 MiB of HBM per device.

v0:
```python
import jax
import jax.numpy as jnp
from jax import lax
from jax.sharding import PartitionSpec as P

BLK = 128


def on_device(tiles, metric, owners):
    fit_count = lax.axis_size("fit")
    tile_rows, pair_count, fit_rows, tile_width = tiles.shape
    occ_slice = tile_width // BLK
    entries = tile_rows * pair_count
    fitted = jnp.einsum("fab,fpbw->fpaw", metric, tiles, preferred_element_type=jnp.float32).astype(
        jnp.bfloat16
    )
    targets = owners.reshape(entries)
    onehot = (targets[:, None] == jnp.arange(fit_count, dtype=jnp.int32)[None, :]).astype(jnp.int32)
    shaped = fitted.reshape(entries, fit_rows, occ_slice, BLK)
    gram_blocks = jnp.einsum("eqia,eqib->eab", shaped, shaped, preferred_element_type=jnp.float32)
    selector = onehot.astype(jnp.float32)
    owner_part = lax.psum_scatter(
        jnp.einsum("ed,eab->dab", selector, gram_blocks, preferred_element_type=jnp.float32),
        "fit",
        scatter_dimension=0,
        tiled=True,
    )[0]
    shares = lax.psum_scatter(owner_part, ("occ", "sub"), scatter_dimension=0, tiled=True)
    return shares[None].astype(jnp.bfloat16)


def solution(mesh):
    placed = (
        P(("grp", "fit"), None, None, ("occ", "sub")),
        P(("grp", "fit"), None, None),
        P(("grp", "fit"), None),
    )
    return jax.shard_map(
        on_device,
        mesh=mesh,
        in_specs=placed,
        out_specs=P(("grp", "fit"), ("occ", "sub"), None),
        check_vma=False,
    )
```

profile of v0, /device:TPU:0, one launch (start us, length us, event | category | flops | bytes accessed | tf_op | source)
XLA Modules:
  0.0 107.6 jit_solution(13776467637608671682)
XLA Ops:
  6.5 0.0 copy-start
  6.5 0.0 reduce-scatter.3.cloned.1.call-start
  6.5 0.9 copy-done
  7.5 12.7 %convolution_convert_fusion = bf16[12,3,4096,64]{2,3,1,0:T(8,128)(2,1)} fusion(bf16[12,3,64,4096]{3,2,1,0:T(8,128)(2,1)} %param.3, bf16[12,64,64]{2,1,0:T(8,128)(2,1)S(1)} %copy-done), kind=kOutput, calls=%fused_computation.2 | convolution fusion | flops 1217396736 | bytes 37847040 | tf_op jit(solution)/shard_map/fab,fpbw->fpaw/dot_general | solution.py:14
  20.2 18.2 %copy.11 = bf16[288,8,32,128]{3,2,1,0:T(8,128)(2,1)} copy(bf16[288,8,32,128]{3,1,2,0:T(8,128)(2,1)} %bitcast.27) | data formatting | bytes 37748736
  38.4 0.0 copy-start.1
  38.4 14.9 %fusion.4 = bf16[36,128,128]{2,1,0:T(8,128)(2,1)S(1)} fusion(bf16[36,64,32,128]{3,2,1,0:T(8,128)(2,1)} %bitcast.28), kind=kOutput, calls=%fused_computation.5 | convolution fusion | flops 2415919104 | bytes 20054016 | tf_op jit(solution)/shard_map/eqia,eqib->eab/dot_general | solution.py:20
  53.3 0.0 copy-done.1
  53.3 0.1 copy.6
  53.4 0.1 eq.15
  53.5 0.9 fusion.2
  54.4 0.9 copy.8
  55.3 0.0 reduce-scatter.3.cloned.1.call-update
  55.3 0.0 reduce-scatter.5.cloned.1.call-start
  55.4 33.8 %reduce-scatter.3.cloned.1.call-done = f32[1,128,128]{2,1,0:T(8,128)} async-done(((f32[8,128,128]{2,1,0:T(8,128)}), f32[1,128,128]{2,1,0:T(8,128)}) %reduce-scatter.3.cloned.1.call-update) | async-done | bytes 65552 | tf_op jit(solution)/shard_map/reduce_scatter | solution.py:22
  89.1 0.0 reduce-scatter.5.cloned.1.call-update
  89.1 10.3 %reduce-scatter.5.cloned.1.call-done = f32[64,128]{1,0:T(8,128)} async-done(((f32[128,128]{1,0:T(8,128)}), f32[64,128]{1,0:T(8,128)}) %reduce-scatter.5.cloned.1.call-update) | async-done | bytes 32784 | tf_op jit(solution)/shard_map/reduce_scatter | solution.py:28
  99.4 1.4 %convert_bitcast_fusion = bf16[1,64,128]{2,1,0:T(8,128)(2,1)} fusion(f32[64,128]{1,0:T(8,128)} %reduce-scatter.5.cloned.1.call-done), kind=kLoop, calls=%fused_computation.7 | loop fusion | flops 8192 | bytes 49152 | tf_op jit(solution)/shard_map/convert_element_type | solution.py:29
Async XLA Ops:
  6.5 0.9 copy-start
  6.5 82.6 %reduce-scatter.3.cloned.1.call-start = ((), (), s32[]{:S(2)}) async-start(), calls=%async_computation.2 | async-start | bytes 589824 | tf_op jit(solution)/shard_map/reduce_scatter | solution.py:22
  38.4 15.0 %copy-start.1 = (s32[12,3]{0,1:T(4,128)S(1)}, s32[12,3]{0,1:T(4,128)}, u32[]{:S(2)}) copy-start(s32[12,3]{0,1:T(4,128)} %param.5) | copy-start | bytes 436
  55.3 44.1 %reduce-scatter.5.cloned.1.call-start = ((), (), s32[]{:S(2)}) async-start(), calls=%async_computation.3 | async-start | bytes 98304 | tf_op jit(solution)/shard_map/reduce_scatter | solution.py:28
Sparse Core Ops, SparseCore 0:
  55.4 33.6 reduce-scatter.2
  91.4 8.0 reduce-scatter.4
where the time goes:
time: 108 us
  waiting for transfers between devices  44.1 us (41%)
  matrix products  28.6 us (26%)
  local copies, waits for them, and re-layouts  20.2 us (19%)
  between operations  13.4 us (12%)
  other arithmetic  1.36 us (1%)
    reduce_scatter x1, waiting for transfers between devices, on_device(): lax.psum_scatter(jnp.einsum('ed,eab->dab', selector, gram_blocks, preferr...  33.8 us
    unnamed x6, local copies, waits for them, and re-layouts  19.2 us
    dot_general x1, matrix products, on_device(): jnp.einsum('eqia,eqib->eab', shaped, shaped, preferred_element_type=jnp.f...  14.9 us
    dot_general x1, matrix products, on_device(): jnp.einsum('fab,fpbw->fpaw', metric, tiles, preferred_element_type=jnp.fl...  12.7 us
    reduce_scatter x1, waiting for transfers between devices, on_device(): lax.psum_scatter(owner_part, ('occ', 'sub'), scatter_dimension=0, tiled=T...  10.3 us
  transfers between devices with their start and end apart: 2, of which 2 were waited for; matrix products, arithmetic and copies ran while one was open for 0% of the time, Pallas kernels for 0%

commit v1 on v0

v1 whole, which is shorter than its diff:
```python
import functools

import jax
import jax.numpy as jnp
from jax import lax
from jax.experimental import pallas as pl
from jax.experimental.pallas import tpu as pltpu
from jax.sharding import PartitionSpec as P

BLK = 128
MESH = pl.DeviceIdType.MESH
OVER_ROWS = (((0,), (0,)), ((), ()))


def each(count, step):
    if count <= 16:
        for k in range(count):
            step(k)
    else:
        lax.fori_loop(0, count, lambda k, carry: (step(k), carry)[1], 0)


def kernel(
    sizes, owners, metric, tiles_hbm, out,
    tiles, acc, send1, recv1, send2, recv2,
    load_sem, send1_sem, recv1_sem, send2_sem, recv2_sem,
):
    fit, occ, sub = sizes
    shards = occ * sub
    tile_rows, pairs, _, width = tiles.shape
    count, rows, _ = send1.shape
    my_fit, my_occ, my_sub = lax.axis_index("fit"), lax.axis_index("occ"), lax.axis_index("sub")

    if sub > 1:
        half = sub // 2
        own_class = lax.rem(my_sub, 2)
        my_slot = (my_fit * occ + my_occ) * half + my_sub // 2
        partner = {"fit": my_fit, "occ": my_occ, "sub": my_sub + 1 - 2 * own_class}

        def place(slot, kind):
            return slot // (occ * half), (slot // half) % occ, (slot % half) * 2 + kind
    else:
        own_class = lax.rem(my_fit, 2)
        my_slot = (my_fit // 2) * occ + my_occ
        partner = {"fit": my_fit + 1 - 2 * own_class, "occ": my_occ, "sub": my_sub}

        def place(slot, kind):
            return (slot // occ) * 2 + kind, slot % occ, 0

    def device_of(slot):
        owner, o, s = place(slot, own_class)
        return {"fit": owner, "occ": o, "sub": s}

    def partial(slot, kind):
        owner, o, s = place(slot, kind)
        return acc[owner, pl.ds(pl.multiple_of((o * sub + s) * rows, rows), rows), :]

    def other(k):
        return lax.rem(my_slot + k, count)

    def load(f):
        return pltpu.make_async_copy(tiles_hbm.at[f], tiles.at[f], load_sem.at[f])

    for f in range(tile_rows):
        load(f).start()

    barrier = pltpu.get_barrier_semaphore()
    pl.semaphore_signal(barrier, inc=1, device_id=partner, device_id_type=MESH)
    each(count - 1, lambda k: pl.semaphore_signal(
        barrier, inc=1, device_id=device_of(other(k + 1)), device_id_type=MESH))

    acc[...] = jnp.zeros_like(acc)
    group = 2 if tile_rows % 2 == 0 else 1

    def work(step, carry):
        members = [step * group + g for g in range(group)]
        for f in members:
            load(f).wait()
        stacked = []
        for f in members:
            for p in range(pairs):
                fitted = jnp.dot(
                    metric[f], tiles[f, p], preferred_element_type=jnp.float32
                ).astype(jnp.bfloat16)
                stacked.append(jnp.concatenate(
                    [fitted[:, c:c + BLK] for c in range(0, width, BLK)], axis=0))
        grams = [
            lax.dot_general(x, x, OVER_ROWS, preferred_element_type=jnp.float32) for x in stacked
        ]
        names = [owners[f, p] for f in members for p in range(pairs)]

        def add(d):
            total = acc[d]
            for name, gram in zip(names, grams):
                total = total + jnp.where(name == d, gram, 0.0)
            acc[d] = total

        for d in range(fit):
            add(d)
        return carry

    lax.fori_loop(0, tile_rows // group, work, 0)

    pl.semaphore_wait(barrier, count)

    def swap(slot):
        return pltpu.make_async_remote_copy(
            src_ref=send1.at[slot], dst_ref=recv1.at[slot],
            send_sem=send1_sem.at[slot], recv_sem=recv1_sem.at[slot],
            device_id=partner, device_id_type=MESH)

    def deliver(slot):
        return pltpu.make_async_remote_copy(
            src_ref=send2.at[slot], dst_ref=recv2.at[my_slot],
            send_sem=send2_sem.at[slot], recv_sem=recv2_sem.at[my_slot],
            device_id=device_of(slot), device_id_type=MESH)

    def arrived(slot):
        return pltpu.make_async_remote_copy(
            src_ref=send2.at[slot], dst_ref=recv2.at[slot],
            send_sem=send2_sem.at[slot], recv_sem=recv2_sem.at[slot],
            device_id=device_of(slot), device_id_type=MESH)

    def give(k):
        slot = other(k + 1)
        send1[slot] = partial(slot, 1 - own_class).astype(jnp.bfloat16)
        swap(slot).start()

    each(count, give)

    def summed(slot):
        swap(slot).wait_recv()
        return partial(slot, own_class) + recv1[slot].astype(jnp.float32)

    def pass_on(k):
        slot = other(k + 1)
        send2[slot] = summed(slot).astype(jnp.bfloat16)
        deliver(slot).start()

    each(count - 1, pass_on)
    total = summed(my_slot)

    def collect(k, total):
        slot = other(count - 1 - k)
        arrived(slot).wait_recv()
        return total + recv2[slot].astype(jnp.float32)

    if count <= 16:
        for k in range(count - 1):
            total = collect(k, total)
    else:
        total = lax.fori_loop(0, count - 1, collect, total)
    out[0] = total.astype(out.dtype)

    each(count, lambda k: swap(other(k + 1)).wait_send())
    each(count - 1, lambda k: deliver(other(k + 1)).wait_send())


def on_device(sizes, tiles, metric, owners):
    fit, occ, sub = sizes
    count = fit * occ * sub // 2
    rows = BLK // (occ * sub)
    tile_rows, pairs, fit_rows, width = tiles.shape
    parts = pltpu.VMEM((count, rows, BLK), jnp.bfloat16)
    return pl.pallas_call(
        functools.partial(kernel, sizes),
        out_shape=jax.ShapeDtypeStruct((1, rows, BLK), jnp.bfloat16),
        in_specs=[
            pl.BlockSpec(memory_space=pltpu.SMEM),
            pl.BlockSpec(memory_space=pltpu.VMEM),
            pl.BlockSpec(memory_space=pl.ANY),
        ],
        out_specs=pl.BlockSpec(memory_space=pltpu.VMEM),
        scratch_shapes=[
            pltpu.VMEM(tiles.shape, jnp.bfloat16),
            pltpu.VMEM((fit, BLK, BLK), jnp.float32),
            parts, parts, parts, parts,
            pltpu.SemaphoreType.DMA((tile_rows,)),
            pltpu.SemaphoreType.DMA((count,)),
            pltpu.SemaphoreType.DMA((count,)),
            pltpu.SemaphoreType.DMA((count,)),
            pltpu.SemaphoreType.DMA((count,)),
        ],
        compiler_params=pltpu.CompilerParams(
            collective_id=0, has_side_effects=True, vmem_limit_bytes=56 << 20
        ),
    )(owners, metric, tiles)


def solution(mesh):
    sizes = tuple(mesh.shape[name] for name in ("fit", "occ", "sub"))
    placed = (
        P(("grp", "fit"), None, None, ("occ", "sub")),
        P(("grp", "fit"), None, None),
        P(("grp", "fit"), None),
    )
    return jax.shard_map(
        functools.partial(on_device, sizes),
        mesh=mesh,
        in_specs=placed,
        out_specs=P(("grp", "fit"), ("occ", "sub"), None),
        check_vma=False,
    )
```

time: 108 us -> 26.2 us (0.24)
  waiting for transfers between devices: 44.1 us -> 0 us
  matrix products: 28.6 us -> 0 us
  Pallas kernels: 0 us -> 23.2 us
  local copies, waits for them, and re-layouts: 20.2 us -> 2.68 us
  between operations: 13.4 us -> 0.01 us
  other arithmetic: 1.36 us -> 0 us
    reduce_scatter x2 -> x0, waiting for transfers between devices: 44 us -> none  [the longest x1 33.8 us: on_device(): lax.psum_scatter(jnp.einsum('ed,eab->dab', selector, gram_blocks, preferr...]
    dot_general x3 -> x0, matrix products: 28.6 us -> none  [the longest x1 14.9 us: on_device(): jnp.einsum('eqia,eqib->eab', shaped, shaped, preferred_element_type=jnp.f...]
    pallas_call x0 -> x1, Pallas kernels: none -> 23.2 us  [on_device(): pl.pallas_call(functools.partial(kernel, sizes), out_shape=jax.ShapeDtype...]
    unnamed x6 -> x2, local copies, waits for them, and re-layouts: 19.2 us -> 2.68 us
    convert_element_type x1 -> x0, other arithmetic: 1.36 us -> none  [on_device(): return shares[None].astype(jnp.bfloat16)]
  transfers between devices with their start and end apart: 2 -> 0, of which waited for: 2 -> 0; matrix products, arithmetic and copies ran while one was open for 0% -> 0% of each run, Pallas kernels for 0% -> 0%
where the time goes in v1:
time: 26.2 us; the launch traced here: 25.9 us
  Pallas kernels  23.2 us (89%)
  local copies, waits for them, and re-layouts  2.68 us (10%)
    pallas_call x1, Pallas kernels, on_device(): pl.pallas_call(functools.partial(kernel, sizes), out_shape=jax.ShapeDtype...  23.2 us
    unnamed x2, local copies, waits for them, and re-layouts  2.68 us

profile of v1, /device:TPU:0, one launch (start us, length us, event | category | flops | bytes accessed | tf_op | source)
XLA Modules:
  0.0 25.9 jit_solution(2007579611320850314)
XLA Ops:
  0.0 1.4 %copy.4.owners = s32[12,3]{1,0:T(8,128)} copy(s32[12,3]{0,1:T(4,128)} %param.5) | data formatting | bytes 288 | tf_op args[2]
  1.4 23.2 %shard_map.37 = bf16[1,64,128]{2,1,0:T(8,128)(2,1)} custom-call(s32[12,3]{1,0:T(8,128)} %copy.4.owners, bf16[12,64,64]{2,1,0:T(8,128)(2,1)} %metric.1, bf16[12,3,64,4096]{3,2,1,0:T(8,128)(2,1)} %tiles_hbm.1), custom_call_target="tpu_custom_call" | custom-call | tf_op jit(solution)/shard_map/pallas_call | solution.py:165
  24.6 1.3 %copy.6 = bf16[1,64,128]{2,1,0:T(8,128)(2,1)} copy(bf16[1,64,128]{2,1,0:T(8,128)(2,1)} %shard_map.37) | data formatting | bytes 32768

commit v2 on v1

--- a/solution.py
+++ b/solution.py
@@ -21,9 +21,9 @@
 
 
 def kernel(
-    sizes, owners, metric, tiles_hbm, out,
-    tiles, acc, send1, recv1, send2, recv2,
-    load_sem, send1_sem, recv1_sem, send2_sem, recv2_sem,
+    sizes, owners_hbm, metric_hbm, tiles_hbm, out,
+    owners, metric, tiles, acc, send1, recv1, send2, recv2,
+    small_sem, load_sem, send1_sem, recv1_sem, send2_sem, recv2_sem,
 ):
     fit, occ, sub = sizes
     shards = occ * sub
@@ -58,11 +58,16 @@
     def other(k):
         return lax.rem(my_slot + k, count)
 
-    def load(f):
-        return pltpu.make_async_copy(tiles_hbm.at[f], tiles.at[f], load_sem.at[f])
-
+    def load(f, p):
+        return pltpu.make_async_copy(tiles_hbm.at[f, p], tiles.at[f, p], load_sem.at[f, p])
+
+    get_metric = pltpu.make_async_copy(metric_hbm, metric, small_sem.at[0])
+    get_owners = pltpu.make_async_copy(owners_hbm, owners, small_sem.at[1])
+    get_metric.start()
+    get_owners.start()
     for f in range(tile_rows):
-        load(f).start()
+        for p in range(pairs):
+            load(f, p).start()
 
     barrier = pltpu.get_barrier_semaphore()
     pl.semaphore_signal(barrier, inc=1, device_id=partner, device_id_type=MESH)
@@ -72,13 +77,17 @@
     acc[...] = jnp.zeros_like(acc)
     group = 2 if tile_rows % 2 == 0 else 1
 
-    def work(step, carry):
+    def work(step, carry, first=False):
         members = [step * group + g for g in range(group)]
-        for f in members:
-            load(f).wait()
         stacked = []
+        if not first:
+            for f in members:
+                for p in range(pairs):
+                    load(f, p).wait()
         for f in members:
             for p in range(pairs):
+                if first:
+                    load(f, p).wait()
                 fitted = jnp.dot(
                     metric[f], tiles[f, p], preferred_element_type=jnp.float32
                 ).astype(jnp.bfloat16)
@@ -87,7 +96,7 @@
         grams = [
             lax.dot_general(x, x, OVER_ROWS, preferred_element_type=jnp.float32) for x in stacked
         ]
-        names = [owners[f, p] for f in members for p in range(pairs)]
+        names = [owners[p, f] for f in members for p in range(pairs)]
 
         def add(d):
             total = acc[d]
@@ -99,7 +108,10 @@
             add(d)
         return carry
 
-    lax.fori_loop(0, tile_rows // group, work, 0)
+    get_metric.wait()
+    get_owners.wait()
+    work(0, 0, first=True)
+    lax.fori_loop(1, tile_rows // group, work, 0)
 
     pl.semaphore_wait(barrier, count)
 
@@ -164,18 +176,21 @@
     parts = pltpu.VMEM((count, rows, BLK), jnp.bfloat16)
     return pl.pallas_call(
         functools.partial(kernel, sizes),
-        out_shape=jax.ShapeDtypeStruct((1, rows, BLK), jnp.bfloat16),
+        out_shape=pltpu.VMEM((1, rows, BLK), jnp.bfloat16),
         in_specs=[
-            pl.BlockSpec(memory_space=pltpu.SMEM),
-            pl.BlockSpec(memory_space=pltpu.VMEM),
+            pl.BlockSpec(memory_space=pl.ANY),
+            pl.BlockSpec(memory_space=pl.ANY),
             pl.BlockSpec(memory_space=pl.ANY),
         ],
         out_specs=pl.BlockSpec(memory_space=pltpu.VMEM),
         scratch_shapes=[
+            pltpu.SMEM((pairs, tile_rows), jnp.int32),
+            pltpu.VMEM(metric.shape, jnp.bfloat16),
             pltpu.VMEM(tiles.shape, jnp.bfloat16),
             pltpu.VMEM((fit, BLK, BLK), jnp.float32),
             parts, parts, parts, parts,
-            pltpu.SemaphoreType.DMA((tile_rows,)),
+            pltpu.SemaphoreType.DMA((2,)),
+            pltpu.SemaphoreType.DMA((tile_rows, pairs)),
             pltpu.SemaphoreType.DMA((count,)),
             pltpu.SemaphoreType.DMA((count,)),
             pltpu.SemaphoreType.DMA((count,)),
@@ -184,7 +199,7 @@
         compiler_params=pltpu.CompilerParams(
             collective_id=0, has_side_effects=True, vmem_limit_bytes=56 << 20
         ),
-    )(owners, metric, tiles)
+    )(owners.T, metric, tiles)
 
 
 def solution(mesh):

time: 26.2 us -> 27.8 us (1.061)
  Pallas kernels: 23.2 us -> 27.1 us
  local copies, waits for them, and re-layouts: 2.68 us -> 0.61 us
    pallas_call x1, Pallas kernels: 23.2 us -> 27.1 us  [on_device(): pl.pallas_call(functools.partial(kernel, sizes), out_shape=pltpu.VMEM((1,...]
    unnamed x2 -> x1, local copies, waits for them, and re-layouts: 2.68 us -> 0.61 us
where the time goes in v2:
time: 27.8 us; the launch traced here: 27.7 us
  Pallas kernels  27.1 us (97%)
  local copies, waits for them, and re-layouts  0.61 us (2%)
    pallas_call x1, Pallas kernels, on_device(): pl.pallas_call(functools.partial(kernel, sizes), out_shape=pltpu.VMEM((1,...  27.1 us
    unnamed x1, local copies, waits for them, and re-layouts  0.61 us

profile of v2, /device:TPU:0, one launch (start us, length us, event | category | flops | bytes accessed | tf_op | source)
XLA Modules:
  0.0 27.7 jit_solution(10798886050596828210)
XLA Ops:
  0.0 27.1 %shard_map.37 = bf16[1,64,128]{2,1,0:T(8,128)(2,1)S(1)} custom-call(s32[3,12]{1,0:T(4,128)} %bitcast.1, bf16[12,64,64]{2,1,0:T(8,128)(2,1)} %metric_hbm.1, bf16[12,3,64,4096]{3,2,1,0:T(8,128)(2,1)} %tiles_hbm.1), custom_call_target="tpu_custom_call" | custom-call | tf_op jit(solution)/shard_map/pallas_call | solution.py:177
  27.1 0.6 %copy.5 = bf16[1,64,128]{2,1,0:T(8,128)(2,1)} copy(bf16[1,64,128]{2,1,0:T(8,128)(2,1)S(1)} %shard_map.37) | data formatting | bytes 32768

commit v3 on v1

--- a/solution.py
+++ b/solution.py
@@ -87,7 +87,7 @@
         grams = [
             lax.dot_general(x, x, OVER_ROWS, preferred_element_type=jnp.float32) for x in stacked
         ]
-        names = [owners[f, p] for f in members for p in range(pairs)]
+        names = [owners[p, f] for f in members for p in range(pairs)]
 
         def add(d):
             total = acc[d]
@@ -164,7 +164,7 @@
     parts = pltpu.VMEM((count, rows, BLK), jnp.bfloat16)
     return pl.pallas_call(
         functools.partial(kernel, sizes),
-        out_shape=jax.ShapeDtypeStruct((1, rows, BLK), jnp.bfloat16),
+        out_shape=pltpu.VMEM((1, rows, BLK), jnp.bfloat16),
         in_specs=[
             pl.BlockSpec(memory_space=pltpu.SMEM),
             pl.BlockSpec(memory_space=pltpu.VMEM),
@@ -184,7 +184,7 @@
         compiler_params=pltpu.CompilerParams(
             collective_id=0, has_side_effects=True, vmem_limit_bytes=56 << 20
         ),
-    )(owners, metric, tiles)
+    )(owners.T, metric, tiles)
 
 
 def solution(mesh):

time: 26.2 us -> 23.5 us (0.90)
  local copies, waits for them, and re-layouts: 2.68 us -> 0.61 us
  Pallas kernels: 23.2 us -> 22.7 us
    unnamed x2 -> x1, local copies, waits for them, and re-layouts: 2.68 us -> 0.61 us
    pallas_call x1, Pallas kernels: 23.2 us -> 22.7 us  [on_device(): pl.pallas_call(functools.partial(kernel, sizes), out_shape=pltpu.VMEM((1,...]
where the time goes in v3:
time: 23.5 us; the launch traced here: 23.3 us
  Pallas kernels  22.7 us (97%)
  local copies, waits for them, and re-layouts  0.61 us (3%)
    pallas_call x1, Pallas kernels, on_device(): pl.pallas_call(functools.partial(kernel, sizes), out_shape=pltpu.VMEM((1,...  22.7 us
    unnamed x1, local copies, waits for them, and re-layouts  0.61 us

profile of v3, /device:TPU:0, one launch (start us, length us, event | category | flops | bytes accessed | tf_op | source)
XLA Modules:
  0.0 23.3 jit_solution(12930337649972274655)
XLA Ops:
  0.0 22.7 %shard_map.37 = bf16[1,64,128]{2,1,0:T(8,128)(2,1)S(1)} custom-call(s32[3,12]{1,0:T(4,128)} %bitcast.1, bf16[12,64,64]{2,1,0:T(8,128)(2,1)} %metric.1, bf16[12,3,64,4096]{3,2,1,0:T(8,128)(2,1)} %tiles_hbm.1), custom_call_target="tpu_custom_call" | custom-call | tf_op jit(solution)/shard_map/pallas_call | solution.py:165
  22.7 0.6 %copy.5 = bf16[1,64,128]{2,1,0:T(8,128)(2,1)} copy(bf16[1,64,128]{2,1,0:T(8,128)(2,1)S(1)} %shard_map.37) | data formatting | bytes 32768
